TPU v7x, 128 devices: a whole 4x4x4 slice. The times are simulated.
128 devices in a mesh: depth: 8 (over z, core), row: 16 (over y, x).
Axes of the slice: x: 4, y: 4, z: 4, core: 2. Of those that a mesh axis runs over, the one named last changes fastest.
Arguments:
- volume: float32 [384, 1024, 2048], P('depth', 'row'), may hold values from -6 to 6
- transfer: float32 [8], replicated, may hold values from 0.3 to 1.2
Outputs:
- image: float32 [4, 1024, 2048], P(None, 'row', 'depth')
All inputs are finite; a program needn't handle non-finite values.
Results may differ from a plain program's by a relative error of at most 0.0003.
Values sent between devices are 32-bit elements; how exact they have to be, the bound alone decides.
A program may use at most 192 MiB of HBM per device.

v0:
```python
import jax
import jax.numpy as jnp
from jax import lax
from jax.sharding import PartitionSpec as P


def with_halo(cells, sides, width):
    for axis, dim in sides:
        count = lax.axis_size(axis)
        ends = count - 1
        head = lax.slice_in_dim(cells, 0, width, axis=dim)
        tail = lax.slice_in_dim(cells, cells.shape[dim] - width, cells.shape[dim], axis=dim)
        cells = jnp.concatenate(
            [
                lax.ppermute(tail, axis, [(i, (i + 1) % count) for i in range(ends)]),
                cells,
                lax.ppermute(head, axis, [((i + 1) % count, i) for i in range(ends)]),
            ],
            axis=dim,
        )
    return cells


def slope_cols(center):
    zero_col = jnp.zeros_like(center[..., :1])
    right = jnp.concatenate([center[..., 1:], zero_col], -1)
    left = jnp.concatenate([zero_col, center[..., :-1]], -1)
    return 0.5 * (right - left)


def emit(framed, transfer, slices):
    center = framed[1:-1, 1:-1, :]
    slope_depth = 0.5 * (framed[2:, 1:-1, :] - framed[:-2, 1:-1, :])
    slope_row = 0.5 * (framed[1:-1, 2:, :] - framed[1:-1, :-2, :])
    slope_col = slope_cols(center)
    inverse = lax.rsqrt(
        slope_depth * slope_depth + slope_row * slope_row + slope_col * slope_col + 1.0
    )
    lambert = jnp.abs((slope_depth + 2.0 * slope_row + 2.0 * slope_col) * inverse) / 3.0
    ambient = 0.5 * transfer[7]
    shading = ambient + (1.0 - ambient) * lambert
    depth_term = 2.0 * transfer[6] / slices * jax.nn.softplus(center)
    opacity = -jnp.expm1(-depth_term)
    tinting = jax.nn.sigmoid(2.0 * center)
    weight = shading * opacity
    emitted = jnp.stack(
        [(transfer[channel] + transfer[3 + channel] * tinting) * weight for channel in range(3)]
    )
    return (emitted, depth_term)


def blend_parts(parts):
    depth_parts = parts[:, 3]
    before = jnp.cumsum(depth_parts, 0) - depth_parts
    color = jnp.sum(jnp.exp(-before)[:, None] * parts[:, :3], 0)
    total = jnp.sum(depth_parts, 0)
    return jnp.concatenate([color, total[None]], 0)


def on_device(volume, transfer):
    local_slices, local_rows, columns = volume.shape
    groups = lax.axis_size("depth")
    slices = local_slices * groups
    padded = with_halo(volume, (("depth", 0), ("row", 1)), 1)
    steps = local_slices // 8

    def march(carry, index):
        color, depth_acc = carry
        slab = lax.dynamic_slice_in_dim(padded, index * 8, 10, 0)
        emitted, depth_term = emit(slab, transfer, slices)
        before = jnp.cumsum(depth_term, 0) - depth_term
        passing = jnp.exp(-(depth_acc[None] + before))
        color = color + jnp.sum(passing[None] * emitted, 1)
        depth_acc = depth_acc + jnp.sum(depth_term, 0)
        return ((color, depth_acc), None)

    start_color = jnp.zeros((3, local_rows, columns), jnp.float32)
    start_depth = jnp.zeros((local_rows, columns), jnp.float32)
    (color, depth_acc), unused = lax.scan(
        march, (start_color, start_depth), jnp.arange(steps, dtype=jnp.int32)
    )
    partial_image = jnp.concatenate([color, depth_acc[None]], 0)
    final = blend_parts(
        lax.all_to_all(partial_image[None], "depth", split_axis=3, concat_axis=0, tiled=True)
    )
    return jnp.concatenate([final[:3], -jnp.expm1(-final[3:4])], 0)


def solution(mesh):
    in_specs = (P("depth", "row", None), P())
    out_specs = P(None, "row", "depth")
    return jax.shard_map(
        on_device, mesh=mesh, in_specs=in_specs, out_specs=out_specs, check_vma=False
    )
```

profile of v0, /device:TPU:14, one launch (start us, length us, event | category | flops | bytes accessed | tf_op | source)
XLA Modules:
  0.0 483.0 jit_solution(13706453914436330940)
XLA Ops:
  4.6 10.6 %constant_dynamic-update-slice_fusion.1 = f32[50,64,2048]{2,1,0:T(8,128)S(1)} fusion(f32[50,64,2048]{2,1,0:T(8,128)S(1)} %constant_dynamic-update-slice_fusion.2, f32[48,64,2048]{2,1,0:T(8,128)} %param.4), kind=kLoop, calls=%fused_computation.28 | loop fusion | bytes 50331648
  36.0 20.7 %pad_maximum_fusion = f32[50,66,2048]{2,1,0:T(8,128)} fusion(f32[50,1,2048]{2,1,0:T(1,128)} %collective-permute-done.3, f32[50,64,2048]{2,1,0:T(8,128)} %copy-done.2, f32[50,1,2048]{2,1,0:T(1,128)S(1)} %collective-permute-done.2), kind=kLoop, calls=%fused_computation.17 | loop fusion | flops 13516800 | bytes 54067200 | tf_op jit(solution)/shard_map/concatenate | solution.py:13
  56.7 343.4 %while.16 = (s32[]{:T(128)}, f32[3,64,2048]{2,1,0:T(8,128)S(1)}, f32[64,2048]{1,0:T(8,128)S(1)}, f32[]{:T(128)}, s32[6]{0:T(128)S(1)}, /*index=5*/f32[50,66,2048...) while((s32[]{:T(128)}, f32[3,64,2048]{2,1,0:T(8,128)S(1)}, ...), condition=%wide.region_4.5_spmd.clone, body=%wide.region_0.4_spmd.clone.sunk | while | flops 86507528 | bytes 139449296 | solution.py:79
  57.8 8.3 %fusion.22 = (f32[8,64,2047]{2,1,0:T(8,128)}, f32[8,64,2047]{2,1,0:T(8,128)}) fusion(f32[50,66,2048]{2,1,0:T(8,128)} %get-tuple-element.322, s32[]{:T(128)S(6)} %add.257, s32[]{:T(128)S(6)} %add.258), kind=kLoop, calls=%fused_computation.31.clone.1 | loop fusion | bytes 16769032 | tf_op jit(solution)/shard_map/while/body/eval_jaxpr/slice | solution.py:26
  66.7 18.1 %multiply_bitcast_fusion.5 = (f32[1,8,64,2048]{3,2,1,0:T(8,128)}, f32[8,64,2048]{2,1,0:T(8,128)S(1)}) fusion(f32[]{:T(128)} %bitcast.41, f32[]{:T(128)} %bitcast.42, f32[50,66,2048]{2,1,0:T(8,128)} %get-tuple-element.322, s32[]{:T(128)S(6)} %add.257, s32[]{:T(128)S(6)} %add.258, f32[]{:T(128)} %get-tuple-element.320, f32[]{:T(128)} %get-tuple-element.325, ...), kind=kLoop, calls=%fused_computation.9.clone.1 | loop fusion | flops 36700160 | bytes 37744680 | tf_op jit(solution)/shard_map/while/body/eval_jaxpr/stack | solution.py:46
  84.9 10.4 %multiply_bitcast_fusion.6 = (f32[1,8,64,2048]{3,2,1,0:T(8,128)}, f32[1,8,64,2048]{3,2,1,0:T(8,128)}, f32[64,2048]{1,0:T(8,128)S(1)}) fusion(f32[8,64,2048]{2,1,0:T(8,128)S(1)} %get-tuple-element.276, f32[]{:T(128)} %bitcast.44, f32[]{:T(128)} %bitcast.45, f32[50,66,2048]{2,1,0:T(8,128)} %get-tuple-element.322, s32[]{:T(128)S(6)} %add.257, ...), kind=kLoop, calls=%fused_computation.8.clone.1 | loop fusion | flops 18743296 | bytes 17301532 | tf_op jit(solution)/shard_map/while/body/eval_jaxpr/stack | solution.py:46
  95.5 12.9 %negate_exponential_fusion.3 = f32[8,64,2048]{2,1,0:T(8,128)S(1)} fusion(f32[64,2048]{1,0:T(8,128)S(1)} %get-tuple-element.285, f32[50,66,2048]{2,1,0:T(8,128)} %get-tuple-element.322, s32[]{:T(128)S(6)} %add.257, s32[]{:T(128)S(6)} %add.258, f32[]{:T(128)} %get-tuple-element.320), kind=kOutput, calls=%fused_computation.12.clone.1 | output fusion | flops 17825792 | bytes 8913416 | tf_op jit(solution)/shard_map/while/body/eval_jaxpr/jit(cumsum)/reduce_window_sum | solution.py:71
  123.0 18.2 %multiply_bitcast_fusion.5 = (f32[1,8,64,2048]{3,2,1,0:T(8,128)}, f32[8,64,2048]{2,1,0:T(8,128)S(1)}) fusion(f32[]{:T(128)} %bitcast.41, f32[]{:T(128)} %bitcast.42, f32[50,66,2048]{2,1,0:T(8,128)} %get-tuple-element.322, s32[]{:T(128)S(6)} %add.257, s32[]{:T(128)S(6)} %add.258, f32[]{:T(128)} %get-tuple-element.320, f32[]{:T(128)} %get-tuple-element.325, ...), kind=kLoop, calls=%fused_computation.9.clone.1 | loop fusion | flops 36700160 | bytes 37744680 | tf_op jit(solution)/shard_map/while/body/eval_jaxpr/stack | solution.py:46
  141.2 10.4 %multiply_bitcast_fusion.6 = (f32[1,8,64,2048]{3,2,1,0:T(8,128)}, f32[1,8,64,2048]{3,2,1,0:T(8,128)}, f32[64,2048]{1,0:T(8,128)S(1)}) fusion(f32[8,64,2048]{2,1,0:T(8,128)S(1)} %get-tuple-element.276, f32[]{:T(128)} %bitcast.44, f32[]{:T(128)} %bitcast.45, f32[50,66,2048]{2,1,0:T(8,128)} %get-tuple-element.322, s32[]{:T(128)S(6)} %add.257, ...), kind=kLoop, calls=%fused_computation.8.clone.1 | loop fusion | flops 18743296 | bytes 17301532 | tf_op jit(solution)/shard_map/while/body/eval_jaxpr/stack | solution.py:46
  151.9 14.1 %negate_exponential_fusion.3 = f32[8,64,2048]{2,1,0:T(8,128)S(1)} fusion(f32[64,2048]{1,0:T(8,128)S(1)} %get-tuple-element.285, f32[50,66,2048]{2,1,0:T(8,128)} %get-tuple-element.322, s32[]{:T(128)S(6)} %add.257, s32[]{:T(128)S(6)} %add.258, f32[]{:T(128)} %get-tuple-element.320), kind=kOutput, calls=%fused_computation.12.clone.1 | output fusion | flops 17825792 | bytes 8913416 | tf_op jit(solution)/shard_map/while/body/eval_jaxpr/jit(cumsum)/reduce_window_sum | solution.py:71
  171.6 8.3 %fusion.22 = (f32[8,64,2047]{2,1,0:T(8,128)}, f32[8,64,2047]{2,1,0:T(8,128)}) fusion(f32[50,66,2048]{2,1,0:T(8,128)} %get-tuple-element.322, s32[]{:T(128)S(6)} %add.257, s32[]{:T(128)S(6)} %add.258), kind=kLoop, calls=%fused_computation.31.clone.1 | loop fusion | bytes 16769032 | tf_op jit(solution)/shard_map/while/body/eval_jaxpr/slice | solution.py:26
  180.6 18.1 %multiply_bitcast_fusion.5 = (f32[1,8,64,2048]{3,2,1,0:T(8,128)}, f32[8,64,2048]{2,1,0:T(8,128)S(1)}) fusion(f32[]{:T(128)} %bitcast.41, f32[]{:T(128)} %bitcast.42, f32[50,66,2048]{2,1,0:T(8,128)} %get-tuple-element.322, s32[]{:T(128)S(6)} %add.257, s32[]{:T(128)S(6)} %add.258, f32[]{:T(128)} %get-tuple-element.320, f32[]{:T(128)} %get-tuple-element.325, ...), kind=kLoop, calls=%fused_computation.9.clone.1 | loop fusion | flops 36700160 | bytes 37744680 | tf_op jit(solution)/shard_map/while/body/eval_jaxpr/stack | solution.py:46
  198.7 10.4 %multiply_bitcast_fusion.6 = (f32[1,8,64,2048]{3,2,1,0:T(8,128)}, f32[1,8,64,2048]{3,2,1,0:T(8,128)}, f32[64,2048]{1,0:T(8,128)S(1)}) fusion(f32[8,64,2048]{2,1,0:T(8,128)S(1)} %get-tuple-element.276, f32[]{:T(128)} %bitcast.44, f32[]{:T(128)} %bitcast.45, f32[50,66,2048]{2,1,0:T(8,128)} %get-tuple-element.322, s32[]{:T(128)S(6)} %add.257, ...), kind=kLoop, calls=%fused_computation.8.clone.1 | loop fusion | flops 18743296 | bytes 17301532 | tf_op jit(solution)/shard_map/while/body/eval_jaxpr/stack | solution.py:46
  209.3 14.2 %negate_exponential_fusion.3 = f32[8,64,2048]{2,1,0:T(8,128)S(1)} fusion(f32[64,2048]{1,0:T(8,128)S(1)} %get-tuple-element.285, f32[50,66,2048]{2,1,0:T(8,128)} %get-tuple-element.322, s32[]{:T(128)S(6)} %add.257, s32[]{:T(128)S(6)} %add.258, f32[]{:T(128)} %get-tuple-element.320), kind=kOutput, calls=%fused_computation.12.clone.1 | output fusion | flops 17825792 | bytes 8913416 | tf_op jit(solution)/shard_map/while/body/eval_jaxpr/jit(cumsum)/reduce_window_sum | solution.py:71
  238.1 17.9 %multiply_bitcast_fusion.5 = (f32[1,8,64,2048]{3,2,1,0:T(8,128)}, f32[8,64,2048]{2,1,0:T(8,128)S(1)}) fusion(f32[]{:T(128)} %bitcast.41, f32[]{:T(128)} %bitcast.42, f32[50,66,2048]{2,1,0:T(8,128)} %get-tuple-element.322, s32[]{:T(128)S(6)} %add.257, s32[]{:T(128)S(6)} %add.258, f32[]{:T(128)} %get-tuple-element.320, f32[]{:T(128)} %get-tuple-element.325, ...), kind=kLoop, calls=%fused_computation.9.clone.1 | loop fusion | flops 36700160 | bytes 37744680 | tf_op jit(solution)/shard_map/while/body/eval_jaxpr/stack | solution.py:46
  256.0 10.4 %multiply_bitcast_fusion.6 = (f32[1,8,64,2048]{3,2,1,0:T(8,128)}, f32[1,8,64,2048]{3,2,1,0:T(8,128)}, f32[64,2048]{1,0:T(8,128)S(1)}) fusion(f32[8,64,2048]{2,1,0:T(8,128)S(1)} %get-tuple-element.276, f32[]{:T(128)} %bitcast.44, f32[]{:T(128)} %bitcast.45, f32[50,66,2048]{2,1,0:T(8,128)} %get-tuple-element.322, s32[]{:T(128)S(6)} %add.257, ...), kind=kLoop, calls=%fused_computation.8.clone.1 | loop fusion | flops 18743296 | bytes 17301532 | tf_op jit(solution)/shard_map/while/body/eval_jaxpr/stack | solution.py:46
  266.6 13.8 %negate_exponential_fusion.3 = f32[8,64,2048]{2,1,0:T(8,128)S(1)} fusion(f32[64,2048]{1,0:T(8,128)S(1)} %get-tuple-element.285, f32[50,66,2048]{2,1,0:T(8,128)} %get-tuple-element.322, s32[]{:T(128)S(6)} %add.257, s32[]{:T(128)S(6)} %add.258, f32[]{:T(128)} %get-tuple-element.320), kind=kOutput, calls=%fused_computation.12.clone.1 | output fusion | flops 17825792 | bytes 8913416 | tf_op jit(solution)/shard_map/while/body/eval_jaxpr/jit(cumsum)/reduce_window_sum | solution.py:71
  295.0 18.2 %multiply_bitcast_fusion.5 = (f32[1,8,64,2048]{3,2,1,0:T(8,128)}, f32[8,64,2048]{2,1,0:T(8,128)S(1)}) fusion(f32[]{:T(128)} %bitcast.41, f32[]{:T(128)} %bitcast.42, f32[50,66,2048]{2,1,0:T(8,128)} %get-tuple-element.322, s32[]{:T(128)S(6)} %add.257, s32[]{:T(128)S(6)} %add.258, f32[]{:T(128)} %get-tuple-element.320, f32[]{:T(128)} %get-tuple-element.325, ...), kind=kLoop, calls=%fused_computation.9.clone.1 | loop fusion | flops 36700160 | bytes 37744680 | tf_op jit(solution)/shard_map/while/body/eval_jaxpr/stack | solution.py:46
  313.3 10.4 %multiply_bitcast_fusion.6 = (f32[1,8,64,2048]{3,2,1,0:T(8,128)}, f32[1,8,64,2048]{3,2,1,0:T(8,128)}, f32[64,2048]{1,0:T(8,128)S(1)}) fusion(f32[8,64,2048]{2,1,0:T(8,128)S(1)} %get-tuple-element.276, f32[]{:T(128)} %bitcast.44, f32[]{:T(128)} %bitcast.45, f32[50,66,2048]{2,1,0:T(8,128)} %get-tuple-element.322, s32[]{:T(128)S(6)} %add.257, ...), kind=kLoop, calls=%fused_computation.8.clone.1 | loop fusion | flops 18743296 | bytes 17301532 | tf_op jit(solution)/shard_map/while/body/eval_jaxpr/stack | solution.py:46
  323.9 14.1 %negate_exponential_fusion.3 = f32[8,64,2048]{2,1,0:T(8,128)S(1)} fusion(f32[64,2048]{1,0:T(8,128)S(1)} %get-tuple-element.285, f32[50,66,2048]{2,1,0:T(8,128)} %get-tuple-element.322, s32[]{:T(128)S(6)} %add.257, s32[]{:T(128)S(6)} %add.258, f32[]{:T(128)} %get-tuple-element.320), kind=kOutput, calls=%fused_computation.12.clone.1 | output fusion | flops 17825792 | bytes 8913416 | tf_op jit(solution)/shard_map/while/body/eval_jaxpr/jit(cumsum)/reduce_window_sum | solution.py:71
  352.6 18.4 %multiply_bitcast_fusion.5 = (f32[1,8,64,2048]{3,2,1,0:T(8,128)}, f32[8,64,2048]{2,1,0:T(8,128)S(1)}) fusion(f32[]{:T(128)} %bitcast.41, f32[]{:T(128)} %bitcast.42, f32[50,66,2048]{2,1,0:T(8,128)} %get-tuple-element.322, s32[]{:T(128)S(6)} %add.257, s32[]{:T(128)S(6)} %add.258, f32[]{:T(128)} %get-tuple-element.320, f32[]{:T(128)} %get-tuple-element.325, ...), kind=kLoop, calls=%fused_computation.9.clone.1 | loop fusion | flops 36700160 | bytes 37744680 | tf_op jit(solution)/shard_map/while/body/eval_jaxpr/stack | solution.py:46
  371.0 10.4 %multiply_bitcast_fusion.6 = (f32[1,8,64,2048]{3,2,1,0:T(8,128)}, f32[1,8,64,2048]{3,2,1,0:T(8,128)}, f32[64,2048]{1,0:T(8,128)S(1)}) fusion(f32[8,64,2048]{2,1,0:T(8,128)S(1)} %get-tuple-element.276, f32[]{:T(128)} %bitcast.44, f32[]{:T(128)} %bitcast.45, f32[50,66,2048]{2,1,0:T(8,128)} %get-tuple-element.322, s32[]{:T(128)S(6)} %add.257, ...), kind=kLoop, calls=%fused_computation.8.clone.1 | loop fusion | flops 18743296 | bytes 17301532 | tf_op jit(solution)/shard_map/while/body/eval_jaxpr/stack | solution.py:46
  381.6 13.9 %negate_exponential_fusion.3 = f32[8,64,2048]{2,1,0:T(8,128)S(1)} fusion(f32[64,2048]{1,0:T(8,128)S(1)} %get-tuple-element.285, f32[50,66,2048]{2,1,0:T(8,128)} %get-tuple-element.322, s32[]{:T(128)S(6)} %add.257, s32[]{:T(128)S(6)} %add.258, f32[]{:T(128)} %get-tuple-element.320), kind=kOutput, calls=%fused_computation.12.clone.1 | output fusion | flops 17825792 | bytes 8913416 | tf_op jit(solution)/shard_map/while/body/eval_jaxpr/jit(cumsum)/reduce_window_sum | solution.py:71
  415.6 42.5 %all_to_all.18 = f32[8,1,65536]{2,1,0:T(1,128)} all-to-all(f32[8,1,65536]{2,1,0:T(1,128)S(1)} %reshape.30), channel_id=1, replica_groups=mesh['depth'=8,'row'=16] {'depth'}, dimensions={0} | all-to-all | bytes 4194304 | tf_op jit(solution)/shard_map/all_to_all | solution.py:84
  (90 shorter events, 132.8 us)
Async XLA Ops:
  1.3 3.3 collective-permute-start
  3.1 12.2 %collective-permute-start.1 = (f32[1,64,2048]{2,1,0:T(8,128)S(1)}, f32[1,64,2048]{2,1,0:T(8,128)S(1)}, u32[]{:S(2)}, u32[]{:S(2)}) collective-permute-start(f32[1,64,2048]{2,1,0:T(8,128)S(1)} %get-tuple-element.196), channel_id=1, source_target_pairs={{16,0},{32,16},{48,32},{64,48},{80,64},{96,80},{112,96},{17,1},{33... | collective-permute-start | bytes 1572872 | tf_op jit(solution)/shard_map/ppermute | solution.py:17
  4.6 22.1 %copy-start.3 = (f32[8]{0:T(128)S(1)}, f32[8]{0:T(128)}, u32[]{:S(2)}) copy-start(f32[8]{0:T(128)} %param.5) | copy-start | bytes 100
  15.3 8.6 %copy-start.2 = (f32[50,64,2048]{2,1,0:T(8,128)}, f32[50,64,2048]{2,1,0:T(8,128)S(1)}, u32[]{:S(2)}) copy-start(f32[50,64,2048]{2,1,0:T(8,128)S(1)} %constant_dynamic-update-slice_fusion) | copy-start | bytes 78643200
  16.1 12.5 %collective-permute-start.2 = (f32[50,1,2048]{2,1,0:T(1,128)S(1)}, f32[50,1,2048]{2,1,0:T(1,128)S(1)}, u32[]{:S(2)}, u32[]{:S(2)}) collective-permute-start(f32[50,1,2048]{2,1,0:T(1,128)S(1)} %get-tuple-element.194), channel_id=1, source_target_pairs={{0,1},{1,2},{2,3},{3,4},{4,5},{5,6},{6,7},{7,8},{8,9},{9,10},{10,1... | collective-permute-start | bytes 1228808 | tf_op jit(solution)/shard_map/ppermute | solution.py:15
  24.0 12.0 %collective-permute-start.3 = (f32[50,1,2048]{2,1,0:T(1,128)S(1)}, f32[50,1,2048]{2,1,0:T(1,128)}, u32[]{:S(2)}, u32[]{:S(2)}) collective-permute-start(f32[50,1,2048]{2,1,0:T(1,128)S(1)} %get-tuple-element.195), channel_id=1, source_target_pairs={{1,0},{2,1},{3,2},{4,3},{5,4},{6,5},{7,6},{8,7},{9,8},{10,9},{11,1... | collective-permute-start | bytes 1228808 | tf_op jit(solution)/shard_map/ppermute | solution.py:17
  95.5 12.9 %copy-start = (f32[1,8,64,2048]{3,2,1,0:T(8,128)S(1)}, f32[1,8,64,2048]{3,2,1,0:T(8,128)}, u32[]{:S(2)}) copy-start(f32[1,8,64,2048]{3,2,1,0:T(8,128)} %get-tuple-element.283) | copy-start | bytes 12582916 | tf_op jit(solution)/shard_map/while
  95.5 12.9 %copy-start.1 = (f32[1,8,64,2048]{3,2,1,0:T(8,128)S(1)}, f32[1,8,64,2048]{3,2,1,0:T(8,128)}, u32[]{:S(2)}) copy-start(f32[1,8,64,2048]{3,2,1,0:T(8,128)} %get-tuple-element.282) | copy-start | bytes 12582916 | tf_op jit(solution)/shard_map/while
  151.8 14.1 %copy-start = (f32[1,8,64,2048]{3,2,1,0:T(8,128)S(1)}, f32[1,8,64,2048]{3,2,1,0:T(8,128)}, u32[]{:S(2)}) copy-start(f32[1,8,64,2048]{3,2,1,0:T(8,128)} %get-tuple-element.283) | copy-start | bytes 12582916 | tf_op jit(solution)/shard_map/while
  151.8 14.1 %copy-start.1 = (f32[1,8,64,2048]{3,2,1,0:T(8,128)S(1)}, f32[1,8,64,2048]{3,2,1,0:T(8,128)}, u32[]{:S(2)}) copy-start(f32[1,8,64,2048]{3,2,1,0:T(8,128)} %get-tuple-element.282) | copy-start | bytes 12582916 | tf_op jit(solution)/shard_map/while
  209.3 14.2 %copy-start = (f32[1,8,64,2048]{3,2,1,0:T(8,128)S(1)}, f32[1,8,64,2048]{3,2,1,0:T(8,128)}, u32[]{:S(2)}) copy-start(f32[1,8,64,2048]{3,2,1,0:T(8,128)} %get-tuple-element.283) | copy-start | bytes 12582916 | tf_op jit(solution)/shard_map/while
  209.3 14.2 %copy-start.1 = (f32[1,8,64,2048]{3,2,1,0:T(8,128)S(1)}, f32[1,8,64,2048]{3,2,1,0:T(8,128)}, u32[]{:S(2)}) copy-start(f32[1,8,64,2048]{3,2,1,0:T(8,128)} %get-tuple-element.282) | copy-start | bytes 12582916 | tf_op jit(solution)/shard_map/while
  266.6 13.8 %copy-start = (f32[1,8,64,2048]{3,2,1,0:T(8,128)S(1)}, f32[1,8,64,2048]{3,2,1,0:T(8,128)}, u32[]{:S(2)}) copy-start(f32[1,8,64,2048]{3,2,1,0:T(8,128)} %get-tuple-element.283) | copy-start | bytes 12582916 | tf_op jit(solution)/shard_map/while
  266.6 13.8 %copy-start.1 = (f32[1,8,64,2048]{3,2,1,0:T(8,128)S(1)}, f32[1,8,64,2048]{3,2,1,0:T(8,128)}, u32[]{:S(2)}) copy-start(f32[1,8,64,2048]{3,2,1,0:T(8,128)} %get-tuple-element.282) | copy-start | bytes 12582916 | tf_op jit(solution)/shard_map/while
  323.9 14.2 %copy-start = (f32[1,8,64,2048]{3,2,1,0:T(8,128)S(1)}, f32[1,8,64,2048]{3,2,1,0:T(8,128)}, u32[]{:S(2)}) copy-start(f32[1,8,64,2048]{3,2,1,0:T(8,128)} %get-tuple-element.283) | copy-start | bytes 12582916 | tf_op jit(solution)/shard_map/while
  323.9 14.2 %copy-start.1 = (f32[1,8,64,2048]{3,2,1,0:T(8,128)S(1)}, f32[1,8,64,2048]{3,2,1,0:T(8,128)}, u32[]{:S(2)}) copy-start(f32[1,8,64,2048]{3,2,1,0:T(8,128)} %get-tuple-element.282) | copy-start | bytes 12582916 | tf_op jit(solution)/shard_map/while
  381.6 13.9 %copy-start = (f32[1,8,64,2048]{3,2,1,0:T(8,128)S(1)}, f32[1,8,64,2048]{3,2,1,0:T(8,128)}, u32[]{:S(2)}) copy-start(f32[1,8,64,2048]{3,2,1,0:T(8,128)} %get-tuple-element.283) | copy-start | bytes 12582916 | tf_op jit(solution)/shard_map/while
  381.6 13.9 %copy-start.1 = (f32[1,8,64,2048]{3,2,1,0:T(8,128)S(1)}, f32[1,8,64,2048]{3,2,1,0:T(8,128)}, u32[]{:S(2)}) copy-start(f32[1,8,64,2048]{3,2,1,0:T(8,128)} %get-tuple-element.282) | copy-start | bytes 12582916 | tf_op jit(solution)/shard_map/while
where the time goes:
time: 484 us; the launch traced here: 483 us
  other arithmetic  327 us (68%)
  local copies, waits for them, and re-layouts  91.4 us (19%)
  blocking collectives  42.5 us (9%)
  starting transfers between devices  9.19 us (2%)
  waiting for transfers between devices  7.54 us (2%)
    another operation x12, other arithmetic, emit(): jnp.stack([(transfer[channel] + transfer[3 + channel] * tinting) * weight...  172 us
    another operation x6, other arithmetic, march(): before = jnp.cumsum(depth_term, 0) - depth_term  83 us
    slice x6, local copies, waits for them, and re-layouts, slope_cols(): right = jnp.concatenate([center[..., 1:], zero_col], -1)  49.7 us
    all_to_all x1, blocking collectives, on_device(): lax.all_to_all(partial_image[None], 'depth', split_axis=3, concat_axis=0,...  42.5 us
    unnamed x8, local copies, waits for them, and re-layouts  26.7 us
    reduce_sum x6, other arithmetic, march(): color = color + jnp.sum(passing[None] * emitted, 1)  23.7 us
    concatenate x1, other arithmetic, with_halo(): jnp.concatenate([lax.ppermute(tail, axis, [(i, (i + 1) % count) for i in...  20.7 us
  transfers between devices with their start and end apart: 4, of which 2 were waited for; matrix products, arithmetic and copies ran while one was open for 2% of the time, Pallas kernels for 0%

commit v1 on v0

--- a/solution.py
+++ b/solution.py
@@ -81,7 +81,15 @@
     )
     partial_image = jnp.concatenate([color, depth_acc[None]], 0)
     final = blend_parts(
-        lax.all_to_all(partial_image[None], "depth", split_axis=3, concat_axis=0, tiled=True)
+        jnp.concatenate(
+            lax.all_to_all(
+                jnp.stack(jnp.split(partial_image[None], lax.axis_size("depth"), axis=3)),
+                "depth",
+                0,
+                0,
+            ),
+            axis=0,
+        )
     )
     return jnp.concatenate([final[:3], -jnp.expm1(-final[3:4])], 0)
 

time: 484 us -> 445 us (0.919)
  other arithmetic: 327 us -> 304 us
  local copies, waits for them, and re-layouts: 91.4 us -> 75.1 us
    unnamed x8 -> x13, local copies, waits for them, and re-layouts: 26.7 us -> 15.3 us
    another operation x1, other arithmetic: 7.68 us -> 0.12 us  [blend_parts(): before = jnp.cumsum(depth_parts, 0) - depth_parts]
    all_to_all x1 -> x0, other arithmetic: 7.22 us -> none  [on_device(): lax.all_to_all(partial_image[None], 'depth', split_axis=3, concat_axis=0,...]
    unnamed x3 -> x2, other arithmetic: 5.27 us -> 0.01 us
  transfers between devices with their start and end apart: 4 -> 4, of which waited for: 2 -> 2; matrix products, arithmetic and copies ran while one was open for 2% -> 3% of each run, Pallas kernels for 0% -> 0%
where the time goes in v1:
time: 445 us; the launch traced here: 444 us
  other arithmetic  304 us (68%)
  local copies, waits for them, and re-layouts  75.1 us (17%)
  blocking collectives  42.4 us (10%)
  starting transfers between devices  9.19 us (2%)
  waiting for transfers between devices  7.54 us (2%)
    another operation x12, other arithmetic, emit(): jnp.stack([(transfer[channel] + transfer[3 + channel] * tinting) * weight...  172 us
    another operation x6, other arithmetic, march(): before = jnp.cumsum(depth_term, 0) - depth_term  83 us
    slice x6, local copies, waits for them, and re-layouts, slope_cols(): right = jnp.concatenate([center[..., 1:], zero_col], -1)  49.7 us
    all_to_all x1, blocking collectives, on_device(): lax.all_to_all(jnp.stack(jnp.split(partial_image[None], lax.axis_size('de...  42.4 us
    reduce_sum x6, other arithmetic, march(): color = color + jnp.sum(passing[None] * emitted, 1)  23.7 us
    concatenate x1, other arithmetic, with_halo(): jnp.concatenate([lax.ppermute(tail, axis, [(i, (i + 1) % count) for i in...  20.7 us
    unnamed x13, local copies, waits for them, and re-layouts  15.3 us
  transfers between devices with their start and end apart: 4, of which 2 were waited for; matrix products, arithmetic and copies ran while one was open for 3% of the time, Pallas kernels for 0%

profile of v1, /device:TPU:14, one launch (start us, length us, event | category | flops | bytes accessed | tf_op | source)
XLA Modules:
  0.0 443.9 jit_solution(1621244166054510542)
XLA Ops:
  4.6 10.6 %constant_dynamic-update-slice_fusion.1 = f32[50,64,2048]{2,1,0:T(8,128)S(1)} fusion(f32[50,64,2048]{2,1,0:T(8,128)S(1)} %constant_dynamic-update-slice_fusion.2, f32[48,64,2048]{2,1,0:T(8,128)} %param.4), kind=kLoop, calls=%fused_computation.46 | loop fusion | bytes 50331648
  36.0 20.7 %pad_maximum_fusion = f32[50,66,2048]{2,1,0:T(8,128)} fusion(f32[50,1,2048]{2,1,0:T(1,128)} %collective-permute-done.3, f32[50,64,2048]{2,1,0:T(8,128)} %copy-done.2, f32[50,1,2048]{2,1,0:T(1,128)S(1)} %collective-permute-done.2), kind=kLoop, calls=%fused_computation.17 | loop fusion | flops 13516800 | bytes 54067200 | tf_op jit(solution)/shard_map/concatenate | solution.py:13
  56.7 343.4 %while.16 = (s32[]{:T(128)}, f32[3,64,2048]{2,1,0:T(8,128)S(1)}, f32[64,2048]{1,0:T(8,128)S(1)}, f32[]{:T(128)}, s32[6]{0:T(128)S(1)}, /*index=5*/f32[50,66,2048...) while((s32[]{:T(128)}, f32[3,64,2048]{2,1,0:T(8,128)S(1)}, ...), condition=%wide.region_4.5_spmd.clone, body=%wide.region_0.4_spmd.clone.sunk | while | flops 86507528 | bytes 139449296 | solution.py:79
  57.8 8.3 %fusion.31 = (f32[8,64,2047]{2,1,0:T(8,128)}, f32[8,64,2047]{2,1,0:T(8,128)}) fusion(f32[50,66,2048]{2,1,0:T(8,128)} %get-tuple-element.320, s32[]{:T(128)S(6)} %add.256, s32[]{:T(128)S(6)} %add.257), kind=kLoop, calls=%fused_computation.49.clone.1 | loop fusion | bytes 16769032 | tf_op jit(solution)/shard_map/while/body/eval_jaxpr/slice | solution.py:26
  66.7 18.1 %multiply_bitcast_fusion.5 = (f32[1,8,64,2048]{3,2,1,0:T(8,128)}, f32[8,64,2048]{2,1,0:T(8,128)S(1)}) fusion(f32[]{:T(128)} %bitcast.66, f32[]{:T(128)} %bitcast.67, f32[50,66,2048]{2,1,0:T(8,128)} %get-tuple-element.320, s32[]{:T(128)S(6)} %add.256, s32[]{:T(128)S(6)} %add.257, f32[]{:T(128)} %get-tuple-element.318, f32[]{:T(128)} %get-tuple-element.323, ...), kind=kLoop, calls=%fused_computation.9.clone.1 | loop fusion | flops 36700160 | bytes 37744680 | tf_op jit(solution)/shard_map/while/body/eval_jaxpr/stack | solution.py:46
  84.9 10.4 %multiply_bitcast_fusion.6 = (f32[1,8,64,2048]{3,2,1,0:T(8,128)}, f32[1,8,64,2048]{3,2,1,0:T(8,128)}, f32[64,2048]{1,0:T(8,128)S(1)}) fusion(f32[8,64,2048]{2,1,0:T(8,128)S(1)} %get-tuple-element.274, f32[]{:T(128)} %bitcast.69, f32[]{:T(128)} %bitcast.70, f32[50,66,2048]{2,1,0:T(8,128)} %get-tuple-element.320, s32[]{:T(128)S(6)} %add.256, ...), kind=kLoop, calls=%fused_computation.8.clone.1 | loop fusion | flops 18743296 | bytes 17301532 | tf_op jit(solution)/shard_map/while/body/eval_jaxpr/stack | solution.py:46
  95.5 12.9 %negate_exponential_fusion.2 = f32[8,64,2048]{2,1,0:T(8,128)S(1)} fusion(f32[64,2048]{1,0:T(8,128)S(1)} %get-tuple-element.283, f32[50,66,2048]{2,1,0:T(8,128)} %get-tuple-element.320, s32[]{:T(128)S(6)} %add.256, s32[]{:T(128)S(6)} %add.257, f32[]{:T(128)} %get-tuple-element.318), kind=kOutput, calls=%fused_computation.12.clone.1 | output fusion | flops 17825792 | bytes 8913416 | tf_op jit(solution)/shard_map/while/body/eval_jaxpr/jit(cumsum)/reduce_window_sum | solution.py:71
  123.0 18.2 %multiply_bitcast_fusion.5 = (f32[1,8,64,2048]{3,2,1,0:T(8,128)}, f32[8,64,2048]{2,1,0:T(8,128)S(1)}) fusion(f32[]{:T(128)} %bitcast.66, f32[]{:T(128)} %bitcast.67, f32[50,66,2048]{2,1,0:T(8,128)} %get-tuple-element.320, s32[]{:T(128)S(6)} %add.256, s32[]{:T(128)S(6)} %add.257, f32[]{:T(128)} %get-tuple-element.318, f32[]{:T(128)} %get-tuple-element.323, ...), kind=kLoop, calls=%fused_computation.9.clone.1 | loop fusion | flops 36700160 | bytes 37744680 | tf_op jit(solution)/shard_map/while/body/eval_jaxpr/stack | solution.py:46
  141.2 10.4 %multiply_bitcast_fusion.6 = (f32[1,8,64,2048]{3,2,1,0:T(8,128)}, f32[1,8,64,2048]{3,2,1,0:T(8,128)}, f32[64,2048]{1,0:T(8,128)S(1)}) fusion(f32[8,64,2048]{2,1,0:T(8,128)S(1)} %get-tuple-element.274, f32[]{:T(128)} %bitcast.69, f32[]{:T(128)} %bitcast.70, f32[50,66,2048]{2,1,0:T(8,128)} %get-tuple-element.320, s32[]{:T(128)S(6)} %add.256, ...), kind=kLoop, calls=%fused_computation.8.clone.1 | loop fusion | flops 18743296 | bytes 17301532 | tf_op jit(solution)/shard_map/while/body/eval_jaxpr/stack | solution.py:46
  151.9 14.1 %negate_exponential_fusion.2 = f32[8,64,2048]{2,1,0:T(8,128)S(1)} fusion(f32[64,2048]{1,0:T(8,128)S(1)} %get-tuple-element.283, f32[50,66,2048]{2,1,0:T(8,128)} %get-tuple-element.320, s32[]{:T(128)S(6)} %add.256, s32[]{:T(128)S(6)} %add.257, f32[]{:T(128)} %get-tuple-element.318), kind=kOutput, calls=%fused_computation.12.clone.1 | output fusion | flops 17825792 | bytes 8913416 | tf_op jit(solution)/shard_map/while/body/eval_jaxpr/jit(cumsum)/reduce_window_sum | solution.py:71
  171.6 8.3 %fusion.31 = (f32[8,64,2047]{2,1,0:T(8,128)}, f32[8,64,2047]{2,1,0:T(8,128)}) fusion(f32[50,66,2048]{2,1,0:T(8,128)} %get-tuple-element.320, s32[]{:T(128)S(6)} %add.256, s32[]{:T(128)S(6)} %add.257), kind=kLoop, calls=%fused_computation.49.clone.1 | loop fusion | bytes 16769032 | tf_op jit(solution)/shard_map/while/body/eval_jaxpr/slice | solution.py:26
  180.6 18.1 %multiply_bitcast_fusion.5 = (f32[1,8,64,2048]{3,2,1,0:T(8,128)}, f32[8,64,2048]{2,1,0:T(8,128)S(1)}) fusion(f32[]{:T(128)} %bitcast.66, f32[]{:T(128)} %bitcast.67, f32[50,66,2048]{2,1,0:T(8,128)} %get-tuple-element.320, s32[]{:T(128)S(6)} %add.256, s32[]{:T(128)S(6)} %add.257, f32[]{:T(128)} %get-tuple-element.318, f32[]{:T(128)} %get-tuple-element.323, ...), kind=kLoop, calls=%fused_computation.9.clone.1 | loop fusion | flops 36700160 | bytes 37744680 | tf_op jit(solution)/shard_map/while/body/eval_jaxpr/stack | solution.py:46
  198.7 10.4 %multiply_bitcast_fusion.6 = (f32[1,8,64,2048]{3,2,1,0:T(8,128)}, f32[1,8,64,2048]{3,2,1,0:T(8,128)}, f32[64,2048]{1,0:T(8,128)S(1)}) fusion(f32[8,64,2048]{2,1,0:T(8,128)S(1)} %get-tuple-element.274, f32[]{:T(128)} %bitcast.69, f32[]{:T(128)} %bitcast.70, f32[50,66,2048]{2,1,0:T(8,128)} %get-tuple-element.320, s32[]{:T(128)S(6)} %add.256, ...), kind=kLoop, calls=%fused_computation.8.clone.1 | loop fusion | flops 18743296 | bytes 17301532 | tf_op jit(solution)/shard_map/while/body/eval_jaxpr/stack | solution.py:46
  209.3 14.2 %negate_exponential_fusion.2 = f32[8,64,2048]{2,1,0:T(8,128)S(1)} fusion(f32[64,2048]{1,0:T(8,128)S(1)} %get-tuple-element.283, f32[50,66,2048]{2,1,0:T(8,128)} %get-tuple-element.320, s32[]{:T(128)S(6)} %add.256, s32[]{:T(128)S(6)} %add.257, f32[]{:T(128)} %get-tuple-element.318), kind=kOutput, calls=%fused_computation.12.clone.1 | output fusion | flops 17825792 | bytes 8913416 | tf_op jit(solution)/shard_map/while/body/eval_jaxpr/jit(cumsum)/reduce_window_sum | solution.py:71
  238.1 17.9 %multiply_bitcast_fusion.5 = (f32[1,8,64,2048]{3,2,1,0:T(8,128)}, f32[8,64,2048]{2,1,0:T(8,128)S(1)}) fusion(f32[]{:T(128)} %bitcast.66, f32[]{:T(128)} %bitcast.67, f32[50,66,2048]{2,1,0:T(8,128)} %get-tuple-element.320, s32[]{:T(128)S(6)} %add.256, s32[]{:T(128)S(6)} %add.257, f32[]{:T(128)} %get-tuple-element.318, f32[]{:T(128)} %get-tuple-element.323, ...), kind=kLoop, calls=%fused_computation.9.clone.1 | loop fusion | flops 36700160 | bytes 37744680 | tf_op jit(solution)/shard_map/while/body/eval_jaxpr/stack | solution.py:46
  256.0 10.4 %multiply_bitcast_fusion.6 = (f32[1,8,64,2048]{3,2,1,0:T(8,128)}, f32[1,8,64,2048]{3,2,1,0:T(8,128)}, f32[64,2048]{1,0:T(8,128)S(1)}) fusion(f32[8,64,2048]{2,1,0:T(8,128)S(1)} %get-tuple-element.274, f32[]{:T(128)} %bitcast.69, f32[]{:T(128)} %bitcast.70, f32[50,66,2048]{2,1,0:T(8,128)} %get-tuple-element.320, s32[]{:T(128)S(6)} %add.256, ...), kind=kLoop, calls=%fused_computation.8.clone.1 | loop fusion | flops 18743296 | bytes 17301532 | tf_op jit(solution)/shard_map/while/body/eval_jaxpr/stack | solution.py:46
  266.6 13.8 %negate_exponential_fusion.2 = f32[8,64,2048]{2,1,0:T(8,128)S(1)} fusion(f32[64,2048]{1,0:T(8,128)S(1)} %get-tuple-element.283, f32[50,66,2048]{2,1,0:T(8,128)} %get-tuple-element.320, s32[]{:T(128)S(6)} %add.256, s32[]{:T(128)S(6)} %add.257, f32[]{:T(128)} %get-tuple-element.318), kind=kOutput, calls=%fused_computation.12.clone.1 | output fusion | flops 17825792 | bytes 8913416 | tf_op jit(solution)/shard_map/while/body/eval_jaxpr/jit(cumsum)/reduce_window_sum | solution.py:71
  295.0 18.2 %multiply_bitcast_fusion.5 = (f32[1,8,64,2048]{3,2,1,0:T(8,128)}, f32[8,64,2048]{2,1,0:T(8,128)S(1)}) fusion(f32[]{:T(128)} %bitcast.66, f32[]{:T(128)} %bitcast.67, f32[50,66,2048]{2,1,0:T(8,128)} %get-tuple-element.320, s32[]{:T(128)S(6)} %add.256, s32[]{:T(128)S(6)} %add.257, f32[]{:T(128)} %get-tuple-element.318, f32[]{:T(128)} %get-tuple-element.323, ...), kind=kLoop, calls=%fused_computation.9.clone.1 | loop fusion | flops 36700160 | bytes 37744680 | tf_op jit(solution)/shard_map/while/body/eval_jaxpr/stack | solution.py:46
  313.3 10.4 %multiply_bitcast_fusion.6 = (f32[1,8,64,2048]{3,2,1,0:T(8,128)}, f32[1,8,64,2048]{3,2,1,0:T(8,128)}, f32[64,2048]{1,0:T(8,128)S(1)}) fusion(f32[8,64,2048]{2,1,0:T(8,128)S(1)} %get-tuple-element.274, f32[]{:T(128)} %bitcast.69, f32[]{:T(128)} %bitcast.70, f32[50,66,2048]{2,1,0:T(8,128)} %get-tuple-element.320, s32[]{:T(128)S(6)} %add.256, ...), kind=kLoop, calls=%fused_computation.8.clone.1 | loop fusion | flops 18743296 | bytes 17301532 | tf_op jit(solution)/shard_map/while/body/eval_jaxpr/stack | solution.py:46
  323.9 14.1 %negate_exponential_fusion.2 = f32[8,64,2048]{2,1,0:T(8,128)S(1)} fusion(f32[64,2048]{1,0:T(8,128)S(1)} %get-tuple-element.283, f32[50,66,2048]{2,1,0:T(8,128)} %get-tuple-element.320, s32[]{:T(128)S(6)} %add.256, s32[]{:T(128)S(6)} %add.257, f32[]{:T(128)} %get-tuple-element.318), kind=kOutput, calls=%fused_computation.12.clone.1 | output fusion | flops 17825792 | bytes 8913416 | tf_op jit(solution)/shard_map/while/body/eval_jaxpr/jit(cumsum)/reduce_window_sum | solution.py:71
  352.6 18.4 %multiply_bitcast_fusion.5 = (f32[1,8,64,2048]{3,2,1,0:T(8,128)}, f32[8,64,2048]{2,1,0:T(8,128)S(1)}) fusion(f32[]{:T(128)} %bitcast.66, f32[]{:T(128)} %bitcast.67, f32[50,66,2048]{2,1,0:T(8,128)} %get-tuple-element.320, s32[]{:T(128)S(6)} %add.256, s32[]{:T(128)S(6)} %add.257, f32[]{:T(128)} %get-tuple-element.318, f32[]{:T(128)} %get-tuple-element.323, ...), kind=kLoop, calls=%fused_computation.9.clone.1 | loop fusion | flops 36700160 | bytes 37744680 | tf_op jit(solution)/shard_map/while/body/eval_jaxpr/stack | solution.py:46
  371.0 10.4 %multiply_bitcast_fusion.6 = (f32[1,8,64,2048]{3,2,1,0:T(8,128)}, f32[1,8,64,2048]{3,2,1,0:T(8,128)}, f32[64,2048]{1,0:T(8,128)S(1)}) fusion(f32[8,64,2048]{2,1,0:T(8,128)S(1)} %get-tuple-element.274, f32[]{:T(128)} %bitcast.69, f32[]{:T(128)} %bitcast.70, f32[50,66,2048]{2,1,0:T(8,128)} %get-tuple-element.320, s32[]{:T(128)S(6)} %add.256, ...), kind=kLoop, calls=%fused_computation.8.clone.1 | loop fusion | flops 18743296 | bytes 17301532 | tf_op jit(solution)/shard_map/while/body/eval_jaxpr/stack | solution.py:46
  381.6 13.9 %negate_exponential_fusion.2 = f32[8,64,2048]{2,1,0:T(8,128)S(1)} fusion(f32[64,2048]{1,0:T(8,128)S(1)} %get-tuple-element.283, f32[50,66,2048]{2,1,0:T(8,128)} %get-tuple-element.320, s32[]{:T(128)S(6)} %add.256, s32[]{:T(128)S(6)} %add.257, f32[]{:T(128)} %get-tuple-element.318), kind=kOutput, calls=%fused_computation.12.clone.1 | output fusion | flops 17825792 | bytes 8913416 | tf_op jit(solution)/shard_map/while/body/eval_jaxpr/jit(cumsum)/reduce_window_sum | solution.py:71
  400.5 42.4 %all_to_all.5 = f32[8,1,4,64,256]{4,3,2,1,0:T(8,128)S(1)} all-to-all(f32[8,1,4,64,256]{4,3,2,1,0:T(8,128)S(1)} %fusion.10), channel_id=1, replica_groups=mesh['depth'=8,'row'=16] {'depth'}, dimensions={0} | all-to-all | bytes 4194304 | tf_op jit(solution)/shard_map/all_to_all | solution.py:85
  (92 shorter events, 93.8 us)
Async XLA Ops:
  1.3 3.3 collective-permute-start
  3.1 12.2 %collective-permute-start.1 = (f32[1,64,2048]{2,1,0:T(8,128)S(1)}, f32[1,64,2048]{2,1,0:T(8,128)S(1)}, u32[]{:S(2)}, u32[]{:S(2)}) collective-permute-start(f32[1,64,2048]{2,1,0:T(8,128)S(1)} %get-tuple-element.196), channel_id=1, source_target_pairs={{16,0},{32,16},{48,32},{64,48},{80,64},{96,80},{112,96},{17,1},{33... | collective-permute-start | bytes 1572872 | tf_op jit(solution)/shard_map/ppermute | solution.py:17
  4.6 22.1 %copy-start.3 = (f32[8]{0:T(128)S(1)}, f32[8]{0:T(128)}, u32[]{:S(2)}) copy-start(f32[8]{0:T(128)} %param.5) | copy-start | bytes 100
  15.3 8.6 %copy-start.2 = (f32[50,64,2048]{2,1,0:T(8,128)}, f32[50,64,2048]{2,1,0:T(8,128)S(1)}, u32[]{:S(2)}) copy-start(f32[50,64,2048]{2,1,0:T(8,128)S(1)} %constant_dynamic-update-slice_fusion) | copy-start | bytes 78643200
  16.1 12.5 %collective-permute-start.2 = (f32[50,1,2048]{2,1,0:T(1,128)S(1)}, f32[50,1,2048]{2,1,0:T(1,128)S(1)}, u32[]{:S(2)}, u32[]{:S(2)}) collective-permute-start(f32[50,1,2048]{2,1,0:T(1,128)S(1)} %get-tuple-element.194), channel_id=1, source_target_pairs={{0,1},{1,2},{2,3},{3,4},{4,5},{5,6},{6,7},{7,8},{8,9},{9,10},{10,1... | collective-permute-start | bytes 1228808 | tf_op jit(solution)/shard_map/ppermute | solution.py:15
  24.0 12.0 %collective-permute-start.3 = (f32[50,1,2048]{2,1,0:T(1,128)S(1)}, f32[50,1,2048]{2,1,0:T(1,128)}, u32[]{:S(2)}, u32[]{:S(2)}) collective-permute-start(f32[50,1,2048]{2,1,0:T(1,128)S(1)} %get-tuple-element.195), channel_id=1, source_target_pairs={{1,0},{2,1},{3,2},{4,3},{5,4},{6,5},{7,6},{8,7},{9,8},{10,9},{11,1... | collective-permute-start | bytes 1228808 | tf_op jit(solution)/shard_map/ppermute | solution.py:17
  95.5 12.9 %copy-start = (f32[1,8,64,2048]{3,2,1,0:T(8,128)S(1)}, f32[1,8,64,2048]{3,2,1,0:T(8,128)}, u32[]{:S(2)}) copy-start(f32[1,8,64,2048]{3,2,1,0:T(8,128)} %get-tuple-element.281) | copy-start | bytes 12582916 | tf_op jit(solution)/shard_map/while
  95.5 12.9 %copy-start.1 = (f32[1,8,64,2048]{3,2,1,0:T(8,128)S(1)}, f32[1,8,64,2048]{3,2,1,0:T(8,128)}, u32[]{:S(2)}) copy-start(f32[1,8,64,2048]{3,2,1,0:T(8,128)} %get-tuple-element.280) | copy-start | bytes 12582916 | tf_op jit(solution)/shard_map/while
  151.8 14.1 %copy-start = (f32[1,8,64,2048]{3,2,1,0:T(8,128)S(1)}, f32[1,8,64,2048]{3,2,1,0:T(8,128)}, u32[]{:S(2)}) copy-start(f32[1,8,64,2048]{3,2,1,0:T(8,128)} %get-tuple-element.281) | copy-start | bytes 12582916 | tf_op jit(solution)/shard_map/while
  151.8 14.1 %copy-start.1 = (f32[1,8,64,2048]{3,2,1,0:T(8,128)S(1)}, f32[1,8,64,2048]{3,2,1,0:T(8,128)}, u32[]{:S(2)}) copy-start(f32[1,8,64,2048]{3,2,1,0:T(8,128)} %get-tuple-element.280) | copy-start | bytes 12582916 | tf_op jit(solution)/shard_map/while
  209.3 14.2 %copy-start = (f32[1,8,64,2048]{3,2,1,0:T(8,128)S(1)}, f32[1,8,64,2048]{3,2,1,0:T(8,128)}, u32[]{:S(2)}) copy-start(f32[1,8,64,2048]{3,2,1,0:T(8,128)} %get-tuple-element.281) | copy-start | bytes 12582916 | tf_op jit(solution)/shard_map/while
  209.3 14.2 %copy-start.1 = (f32[1,8,64,2048]{3,2,1,0:T(8,128)S(1)}, f32[1,8,64,2048]{3,2,1,0:T(8,128)}, u32[]{:S(2)}) copy-start(f32[1,8,64,2048]{3,2,1,0:T(8,128)} %get-tuple-element.280) | copy-start | bytes 12582916 | tf_op jit(solution)/shard_map/while
  266.6 13.8 %copy-start = (f32[1,8,64,2048]{3,2,1,0:T(8,128)S(1)}, f32[1,8,64,2048]{3,2,1,0:T(8,128)}, u32[]{:S(2)}) copy-start(f32[1,8,64,2048]{3,2,1,0:T(8,128)} %get-tuple-element.281) | copy-start | bytes 12582916 | tf_op jit(solution)/shard_map/while
  266.6 13.8 %copy-start.1 = (f32[1,8,64,2048]{3,2,1,0:T(8,128)S(1)}, f32[1,8,64,2048]{3,2,1,0:T(8,128)}, u32[]{:S(2)}) copy-start(f32[1,8,64,2048]{3,2,1,0:T(8,128)} %get-tuple-element.280) | copy-start | bytes 12582916 | tf_op jit(solution)/shard_map/while
  323.9 14.2 %copy-start = (f32[1,8,64,2048]{3,2,1,0:T(8,128)S(1)}, f32[1,8,64,2048]{3,2,1,0:T(8,128)}, u32[]{:S(2)}) copy-start(f32[1,8,64,2048]{3,2,1,0:T(8,128)} %get-tuple-element.281) | copy-start | bytes 12582916 | tf_op jit(solution)/shard_map/while
  323.9 14.2 %copy-start.1 = (f32[1,8,64,2048]{3,2,1,0:T(8,128)S(1)}, f32[1,8,64,2048]{3,2,1,0:T(8,128)}, u32[]{:S(2)}) copy-start(f32[1,8,64,2048]{3,2,1,0:T(8,128)} %get-tuple-element.280) | copy-start | bytes 12582916 | tf_op jit(solution)/shard_map/while
  381.6 13.9 %copy-start = (f32[1,8,64,2048]{3,2,1,0:T(8,128)S(1)}, f32[1,8,64,2048]{3,2,1,0:T(8,128)}, u32[]{:S(2)}) copy-start(f32[1,8,64,2048]{3,2,1,0:T(8,128)} %get-tuple-element.281) | copy-start | bytes 12582916 | tf_op jit(solution)/shard_map/while
  381.6 13.9 %copy-start.1 = (f32[1,8,64,2048]{3,2,1,0:T(8,128)S(1)}, f32[1,8,64,2048]{3,2,1,0:T(8,128)}, u32[]{:S(2)}) copy-start(f32[1,8,64,2048]{3,2,1,0:T(8,128)} %get-tuple-element.280) | copy-start | bytes 12582916 | tf_op jit(solution)/shard_map/while
